TPU v7x, 32 devices: a whole 2x2x4 slice. The times are simulated.
32 devices in a mesh: row: 2 (over y), col: 4 (over x, core), layer: 4 (over z).
Axes of the slice: x: 2, y: 2, z: 4, core: 2. Of those that a mesh axis runs over, the one named last changes fastest.
Arguments:
- panel: bfloat16 [2048, 4, 1024], P('row', 'layer', 'col'), may hold values from -6 to 6
- in_pattern: int32 [16, 4, 8], P('row', 'layer', 'col'), may hold values 0 or 1
- slab: bfloat16 [4, 8, 128, 2048], P('layer', 'row', None, 'col'), may hold values from -0.09375 to 0.09375
- owner: int32 [4, 8], P('layer'), may hold values from 0 to 7, each once within a row
- out_pattern: int32 [16, 16], P(('row', 'layer'), 'col'), may hold values 0 or 1
Outputs:
- product: bfloat16 [2048, 2048], P(('row', 'layer'), 'col')
Inputs may be any that keep to these rules, and one draw needn't show every extreme that they name: `owner`: each row lists every number of 0 to 7 once.
All inputs are finite; a program needn't handle non-finite values. No bound on the sum of `in_pattern` or of `out_pattern` on one device may be relied on, other than what follows from the above.
Results may differ from a plain program's by a relative error of at most 0.001.
Values may be sent and summed in bfloat16 or wider, within the bound.
A program may use at most 64 MiB of HBM per device.

v0:
```python
import jax
import jax.numpy as jnp
from jax import lax
from jax.sharding import PartitionSpec as P


def shards(panel, in_pattern, slab, owner, out_pattern):
    block_size = slab.shape[2]
    slab_cols = slab.shape[3]
    panel_rows = panel.shape[0]
    local_blocks = in_pattern.shape[2]
    shaped = panel.reshape(in_pattern.shape[0], block_size, 1, local_blocks, block_size)
    keeper = in_pattern.astype(jnp.bfloat16)[:, None, :, :, None]
    masked = (shaped * keeper).reshape(panel_rows, 1, local_blocks * block_size)
    mapping = owner[0]
    range_rows = lax.all_gather(slab, "row", axis=1, tiled=True)[0]
    portion = lax.all_gather(masked, "col", axis=2, tiled=True)
    amount = portion.shape[2] // block_size
    operand = jnp.take(range_rows, mapping, axis=0).reshape(amount * block_size, slab_cols)
    summed = jnp.dot(portion[:, 0, :], operand, preferred_element_type=jnp.float32)
    reduced = lax.psum_scatter(summed, "layer", scatter_dimension=0, tiled=True)
    out_rows = out_pattern.shape[0]
    out_cols = out_pattern.shape[1]
    blocked = reduced.reshape(out_rows, block_size, out_cols, block_size)
    blocked = blocked * out_pattern.astype(jnp.float32)[:, None, :, None]
    return blocked.reshape(out_rows * block_size, out_cols * block_size).astype(jnp.bfloat16)


def solution(mesh):
    in_specs = (
        P("row", "layer", "col"),
        P("row", "layer", "col"),
        P("layer", "row", None, "col"),
        P("layer", None),
        P(("row", "layer"), "col"),
    )
    out_specs = P(("row", "layer"), "col")
    return jax.shard_map(shards, mesh=mesh, in_specs=in_specs, out_specs=out_specs, check_vma=False)
```

profile of v0, /device:TPU:0, one launch (start us, length us, event | category | flops | bytes accessed | tf_op | source)
XLA Modules:
  0.0 114.1 jit_solution(15379711690204778151)
XLA Ops:
  6.5 0.0 copy-start
  6.5 0.0 all-gather.5.cloned.1.call-start
  6.5 0.0 copy-start.2
  6.5 0.7 all-gather.5.cloned.1.call-update
  7.3 0.0 all-gather.3.cloned.1.call-start
  7.3 0.7 convert_bitcast_fusion
  8.0 0.1 copy.7
  8.1 0.3 mul.27
  8.4 0.3 mul.28
  8.8 0.0 copy-done
  8.8 0.9 mul.29
  9.7 0.0 all-gather.3.cloned.1.call-update
  9.7 0.0 reduce-scatter.2.cloned.1.call-start
  9.8 0.0 copy-done.2
  9.8 23.1 %all-gather.5.cloned.1.call-done = bf16[1,8,128,512]{3,2,0,1:T(8,128)(2,1)} async-done(((bf16[1,4,128,512]{3,2,0,1:T(8,128)(2,1)}), bf16[1,8,128,512]{3,2,0,1:T(8,128)(2,1)}) %all-gather.5.cloned.1.call-update) | async-done | bytes 1048592 | tf_op jit(solution)/shard_map/all_gather | solution.py:16
  32.9 1.8 %gather_fusion = bf16[8,128,512]{2,1,0:T(8,128)(2,1)S(1)} fusion(bf16[8,128,512]{2,1,0:T(8,128)(2,1)} %bitcast.22, s32[1024]{0:T(1024)S(1)} %pad_clamp_fusion), kind=kCustom, calls=%fused_computation | custom fusion | bytes 2097184 | tf_op jit(solution)/shard_map/jit(_take)/gather | solution.py:19
  34.8 0.2 broadcast_select_fusion
  35.0 22.4 %all-gather.3.cloned.1.call-done = bf16[1024,1,1024]{2,0,1:T(8,128)(2,1)} async-done(((bf16[1024,1,256]{2,0,1:T(8,128)(2,1)}), bf16[1024,1,1024]{2,0,1:T(8,128)(2,1)}) %all-gather.3.cloned.1.call-update) | async-done | bytes 2097168 | tf_op jit(solution)/shard_map/all_gather | solution.py:17
  57.4 4.2 %fusion = f32[1024,512]{1,0:T(8,128)} fusion(bf16[1024,512]{1,0:T(8,128)(2,1)S(1)} %bitcast.23, bf16[1024,1,1024]{2,0,1:T(8,128)(2,1)} %all-gather.3.cloned.1.call-done), kind=kOutput, calls=%fused_computation.1 | convolution fusion | flops 1073741824 | bytes 5242880 | tf_op jit(solution)/shard_map/dot_general | solution.py:20
  61.5 0.0 copy-start.1
  61.5 0.0 reduce-scatter.2.cloned.1.call-update
  61.6 0.7 copy-done.1
  62.2 43.4 %reduce-scatter.2.cloned.1.call-done = f32[256,512]{1,0:T(8,128)} async-done(((f32[1024,512]{1,0:T(8,128)}), f32[256,512]{1,0:T(8,128)}) %reduce-scatter.2.cloned.1.call-update) | async-done | bytes 524304 | tf_op jit(solution)/shard_map/reduce_scatter | solution.py:21
  105.6 0.1 mul.30
  105.7 1.8 %fusion.2 = bf16[256,512]{1,0:T(8,128)(2,1)} fusion(f32[256,512]{1,0:T(8,128)} %reduce-scatter.2.cloned.1.call-done, f32[32,8,4,128]{3,2,1,0:T(4,128)S(1)} %bitcast.21), kind=kLoop, calls=%fused_computation.5 | loop fusion | flops 262144 | bytes 1310720 | tf_op jit(solution)/shard_map/convert_element_type | solution.py:26
  (4 shorter events, 0.0 us)
Async XLA Ops:
  6.5 2.2 %copy-start = (bf16[1024,1,256]{2,0,1:T(8,128)(2,1)S(1)}, bf16[1024,1,256]{2,0,1:T(8,128)(2,1)}, u32[]{:S(2)}) copy-start(bf16[1024,1,256]{2,0,1:T(8,128)(2,1)} %param.5) | copy-start | bytes 1572868
  6.5 26.4 %all-gather.5.cloned.1.call-start = ((), (), s32[]{:S(2)}) async-start(), calls=%async_computation.2 | async-start | bytes 1572864 | tf_op jit(solution)/shard_map/all_gather | solution.py:16
  6.5 3.2 %copy-start.2 = (s32[1,8]{1,0:T(1,128)S(1)}, s32[1,8]{1,0:T(1,128)}, u32[]{:S(2)}) copy-start(s32[1,8]{1,0:T(1,128)} %param.8) | copy-start | bytes 100
  7.3 50.1 %all-gather.3.cloned.1.call-start = ((), (), s32[]{:S(2)}) async-start(), calls=%async_computation.1 | async-start | bytes 2621440 | tf_op jit(solution)/shard_map/all_gather | solution.py:17
  9.7 95.9 %reduce-scatter.2.cloned.1.call-start = ((), (), s32[]{:S(2)}) async-start(), calls=%async_computation.3 | async-start | bytes 2621440 | tf_op jit(solution)/shard_map/reduce_scatter | solution.py:21
  61.5 0.7 copy-start.1
Sparse Core Ops, SparseCore 0:
  8.9 23.9 all-gather.4
  34.5 22.8 all-gather.2
  61.7 43.8 reduce-scatter.1
where the time goes:
time: 114 us
  waiting for transfers between devices  89.6 us (79%)
  between operations  13.2 us (12%)
  matrix products  4.17 us (4%)
  other arithmetic  3.61 us (3%)
  local copies, waits for them, and re-layouts  3.4 us (3%)
    reduce_scatter x1, waiting for transfers between devices, shards(): reduced = lax.psum_scatter(summed, 'layer', scatter_dimension=0, tiled=True)  43.4 us
    all_gather x1, waiting for transfers between devices, shards(): range_rows = lax.all_gather(slab, 'row', axis=1, tiled=True)[0]  23.1 us
    all_gather x1, waiting for transfers between devices, shards(): portion = lax.all_gather(masked, 'col', axis=2, tiled=True)  22.4 us
    dot_general x1, matrix products, shards(): jnp.dot(portion[:, 0, :], operand, preferred_element_type=jnp.float32)  4.17 us
  transfers between devices with their start and end apart: 3, of which 3 were waited for; matrix products, arithmetic and copies ran while one was open for 4% of the time, Pallas kernels for 0%

commit v1 on v0

v1 whole, which is shorter than its diff:
```python
import functools

import jax
import jax.numpy as jnp
from jax import lax
from jax.experimental import pallas as pl
from jax.experimental.pallas import tpu as pltpu
from jax.sharding import PartitionSpec as P

MESH = pl.DeviceIdType.MESH
STEPS = 128.0
TOP = 32640.0
PAD = 16


def encode(values, out):
    rows = values.shape[0]
    peak = jnp.maximum(jnp.max(jnp.abs(values), axis=0, keepdims=True), 2.0**-100)
    level = jnp.ceil(jnp.log2(peak) * STEPS + 0.5)
    factor = jnp.exp2(level * (-1.0 / STEPS)) * TOP
    coded = jnp.round(values * factor).astype(jnp.int32)
    out[0:rows, :] = coded.astype(jnp.int16)
    wide = jnp.broadcast_to(level, (PAD, values.shape[1]))
    out[rows : rows + PAD, :] = wide.astype(jnp.int32).astype(jnp.int16)


def decode(message, rows):
    level = message[rows : rows + PAD, :].astype(jnp.int32).astype(jnp.float32)[0:1, :]
    factor = jnp.exp2(level * (1.0 / STEPS)) * (1.0 / TOP)
    return message[0:rows, :].astype(jnp.int32).astype(jnp.float32) * factor


def kernel(sizes, panel, in_pat, slab, owner, out_pat, out, *scratch):
    R, C, L, N = sizes
    slabs, ops = scratch[:N], scratch[N : 2 * N]
    portion, sbuf, rbuf, acc, sx, sc, sr, rp, ss, rs, sz, rz = scratch[2 * N :]
    H = C // 2
    row, col, z = lax.axis_index("row"), lax.axis_index("col"), lax.axis_index("layer")
    half, side = col // 2, col % 2
    mate = half * 2 + (1 - side)
    rows = out.shape[0]
    bs = slab.shape[2]
    depth = panel.shape[2]
    wide = out.shape[1] // N
    mine = slab.shape[1]
    brows = rows // bs
    hops = [((half + i) % H) * 2 + side for i in range(1, H)]
    relays = [((half + i) % H) * 2 + (1 - side) for i in range(1, H)]
    peers = [(row + i) % R for i in range(1, R)]

    barrier = pltpu.get_barrier_semaphore()
    for c in hops + [mate]:
        pl.semaphore_signal(barrier, inc=1, device_id={"col": c}, device_id_type=MESH)
    for r in peers:
        pl.semaphore_signal(barrier, inc=1, device_id={"row": r}, device_id_type=MESH)

    @pl.when(z > 0)
    def _():
        pl.semaphore_signal(barrier, inc=1, device_id={"layer": z - 1}, device_id_type=MESH)

    @pl.when(z < L - 1)
    def _():
        pl.semaphore_signal(barrier, inc=1, device_id={"layer": z + 1}, device_id_type=MESH)

    tables = [sorted(range(L), key=lambda d: (-abs(d - i), d)) for i in range(L)]

    def pick(t):
        found = 0
        for i in range(L):
            found = found + jnp.where(z == i, tables[i][t], 0)
        return found

    dest = [pick(t) for t in range(L)]

    def mask(t):
        for i in range(brows):
            first = pl.multiple_of(dest[t] * rows + i * bs, bs)
            for j in range(depth // bs):
                keep = in_pat[dest[t] * brows + i, 0, j].astype(jnp.float32)
                block = panel[pl.ds(first, bs), 0, j * bs : (j + 1) * bs].astype(jnp.float32)
                portion[col, t, i * bs : (i + 1) * bs, j * bs : (j + 1) * bs] = (block * keep).astype(jnp.bfloat16)

    def send_part(c_to, t, sem):
        return pltpu.make_async_remote_copy(
            src_ref=portion.at[col, t], dst_ref=portion.at[col, t], send_sem=sem, recv_sem=rp.at[col, t],
            device_id={"col": c_to}, device_id_type=MESH)

    def relay(c_from, t, sem):
        return pltpu.make_async_remote_copy(
            src_ref=portion.at[c_from, t], dst_ref=portion.at[c_from, t], send_sem=sem, recv_sem=rp.at[c_from, t],
            device_id={"col": mate}, device_id_type=MESH)

    def send_slab(r_to, i, n):
        return pltpu.make_async_remote_copy(
            src_ref=slab.at[0, :, :, pl.ds(n * wide, wide)], dst_ref=slabs[n].at[pl.ds(row * mine, mine)],
            send_sem=ss.at[i, n], recv_sem=rs.at[row, n], device_id={"row": r_to}, device_id_type=MESH)

    def start_parts(t):
        for i, c in enumerate(hops):
            send_part(c, t, sx.at[i, t]).start()
        send_part(mate, t, sc.at[t]).start()

    def start_slab(n):
        for i, r in enumerate(peers):
            send_slab(r, i, n).start()

    mask(0)
    pl.semaphore_wait(barrier, (R - 1) + H + jnp.where(z > 0, 1, 0) + jnp.where(z < L - 1, 1, 0))
    start_slab(0)
    start_parts(0)
    for t in range(1, L):
        mask(t)
        start_parts(t)
    for n in range(1, N):
        start_slab(n)
    for n in range(N):
        slabs[n][pl.ds(row * mine, mine)] = slab[0, :, :, n * wide : (n + 1) * wide]

    def ready_parts(t):
        for i, c in enumerate(hops):
            relay(c, t, sr.at[i, t]).wait_recv()
            relay(c, t, sr.at[i, t]).start()

    def wait_parts(t):
        for c in [mate] + relays:
            relay(c, t, sc.at[t]).wait_recv()

    def ready_slab(n):
        for r in peers:
            pltpu.make_async_remote_copy(
                src_ref=slabs[n].at[pl.ds(r * mine, mine)], dst_ref=slabs[n].at[pl.ds(r * mine, mine)],
                send_sem=ss.at[0, n], recv_sem=rs.at[r, n], device_id={"row": r}, device_id_type=MESH).wait_recv()
        for j in range(R * mine):
            ops[n][j * bs : (j + 1) * bs, :] = slabs[n][owner[0, j]]

    def product(t, n):
        total = jnp.dot(portion[0, t], ops[n][0:depth, :], preferred_element_type=jnp.float32)
        for c in range(1, C):
            total += jnp.dot(portion[c, t], ops[n][c * depth : (c + 1) * depth, :], preferred_element_type=jnp.float32)
        return total

    def message(t, n, slot, to):
        return pltpu.make_async_remote_copy(
            src_ref=sbuf.at[t, n], dst_ref=rbuf.at[slot, n], send_sem=sz.at[t, n], recv_sem=rz.at[slot, n],
            device_id={"layer": to}, device_id_type=MESH)

    def arrived(slot, n):
        message(0, n, slot, (z + 1) % L).wait_recv()
        return decode(rbuf.at[slot, n], rows)

    def route(t):
        up = jnp.where(dest[t] > z, 1, 0)
        return dest[t] + L * (1 - up), z + 2 * up - 1

    for n in range(N):
        for t in range(L - 1):
            if n == 0:
                ready_parts(t)
                if t == 0:
                    ready_slab(0)
                wait_parts(t)
            elif t == 0:
                ready_slab(n)
            slot, to = route(t)
            inner = (z > 0) & (z < L - 1)

            @pl.when(inner)
            def _(t=t, n=n, slot=slot):
                total = product(t, n)
                encode(total + arrived(slot, n), sbuf.at[t, n])

            @pl.when(jnp.logical_not(inner))
            def _(t=t, n=n):
                encode(product(t, n), sbuf.at[t, n])

            message(t, n, slot, to).start()

    ready_parts(L - 1)
    wait_parts(L - 1)
    for n in range(N):
        acc[:, n * wide : (n + 1) * wide] = product(L - 1, n)
    for n in range(N):
        here = slice(n * wide, (n + 1) * wide)

        @pl.when(z > 0)
        def _():
            acc[:, here] += arrived(z, n)

        @pl.when(z < L - 1)
        def _():
            acc[:, here] += arrived(z + L, n)

        for i in range(brows):
            for j in range(n * wide // bs, (n + 1) * wide // bs):
                keep = out_pat[i, j].astype(jnp.float32)
                at = (slice(i * bs, (i + 1) * bs), slice(j * bs, (j + 1) * bs))
                out[at] = (acc[at] * keep).astype(jnp.bfloat16)

    for t in range(L):
        for i, c in enumerate(hops):
            send_part(c, t, sx.at[i, t]).wait_send()
            relay(c, t, sr.at[i, t]).wait_send()
        send_part(mate, t, sc.at[t]).wait_send()
    for n in range(N):
        for i, r in enumerate(peers):
            send_slab(r, i, n).wait_send()
        for t in range(L - 1):
            slot, to = route(t)
            message(t, n, slot, to).wait_send()


def solution(mesh):
    R, C, L = (mesh.shape[name] for name in ("row", "col", "layer"))
    N = 2

    def shards(panel, in_pat, slab, owner, out_pat):
        bs, cols = slab.shape[2], slab.shape[3]
        rows = panel.shape[0] // L
        depth = panel.shape[2]
        blocks = R * slab.shape[1]
        wide = cols // N
        H = C // 2
        dma = pltpu.SemaphoreType.DMA
        vmem = pl.BlockSpec(memory_space=pltpu.VMEM)
        smem = pl.BlockSpec(memory_space=pltpu.SMEM)
        return pl.pallas_call(
            functools.partial(kernel, (R, C, L, N)),
            out_shape=jax.ShapeDtypeStruct((rows, cols), jnp.bfloat16),
            in_specs=[vmem, smem, vmem, smem, smem],
            out_specs=vmem,
            scratch_shapes=[pltpu.VMEM((blocks, bs, wide), jnp.bfloat16) for _ in range(N)]
            + [pltpu.VMEM((blocks * bs, wide), jnp.bfloat16) for _ in range(N)]
            + [
                pltpu.VMEM((C, L, rows, depth), jnp.bfloat16),
                pltpu.VMEM((L - 1, N, rows + PAD, wide), jnp.int16),
                pltpu.VMEM((2 * L, N, rows + PAD, wide), jnp.int16),
                pltpu.VMEM((rows, cols), jnp.float32),
                dma((H - 1, L)),
                dma((L,)),
                dma((H - 1, L)),
                dma((C, L)),
                dma((R - 1, N)),
                dma((R, N)),
                dma((L - 1, N)),
                dma((2 * L, N)),
            ],
            compiler_params=pltpu.CompilerParams(
                collective_id=0, has_side_effects=True, vmem_limit_bytes=48 * 2**20),
        )(panel, in_pat, slab, owner, out_pat)

    in_specs = (
        P("row", "layer", "col"),
        P("row", "layer", "col"),
        P("layer", "row", None, "col"),
        P("layer", None),
        P(("row", "layer"), "col"),
    )
    out_specs = P(("row", "layer"), "col")
    return jax.shard_map(shards, mesh=mesh, in_specs=in_specs, out_specs=out_specs, check_vma=False)
```

time: 114 us -> 40.3 us (0.35)
  waiting for transfers between devices: 89.6 us -> 0 us
  Pallas kernels: 0 us -> 36.7 us
  between operations: 13.2 us -> 0.04 us
  matrix products: 4.17 us -> 0 us
  other arithmetic: 3.61 us -> 0 us
    all_gather x2 -> x0, waiting for transfers between devices: 45.5 us -> none  [the longest x1 23.1 us: shards(): range_rows = lax.all_gather(slab, 'row', axis=1, tiled=True)[0]]
    reduce_scatter x1 -> x0, waiting for transfers between devices: 43.4 us -> none  [shards(): reduced = lax.psum_scatter(summed, 'layer', scatter_dimension=0, tiled=True)]
    pallas_call x0 -> x1, Pallas kernels: none -> 36.7 us  [shards(): pl.pallas_call(functools.partial(kernel, (R, C, L, N)), out_shape=jax.Sha...]
    dot_general x1 -> x0, matrix products: 4.17 us -> none  [shards(): jnp.dot(portion[:, 0, :], operand, preferred_element_type=jnp.float32)]
    unnamed x6 -> x9, local copies, waits for them, and re-layouts: 0.66 us -> 3.38 us
    gather x1 -> x0, local copies, waits for them, and re-layouts: 1.84 us -> none  [shards(): jnp.take(range_rows, mapping, axis=0)]
    convert_element_type x2 -> x0, other arithmetic: 1.82 us -> none  [the longest x1 1.82 us: shards(): blocked.reshape(out_rows * block_size, out_cols * block_size)]
    mul x2 -> x0, other arithmetic: 1.61 us -> none  [shards(): masked = (shaped * keeper).reshape(panel_rows, 1, local_blocks * block_size)]
  transfers between devices with their start and end apart: 3 -> 0, of which waited for: 3 -> 0; matrix products, arithmetic and copies ran while one was open for 4% -> 0% of each run, Pallas kernels for 0% -> 0%
where the time goes in v1:
time: 40.3 us; the launch traced here: 40.1 us
  Pallas kernels  36.7 us (91%)
  local copies, waits for them, and re-layouts  3.38 us (8%)
    pallas_call x1, Pallas kernels, shards(): pl.pallas_call(functools.partial(kernel, (R, C, L, N)), out_shape=jax.Sha...  36.7 us
    unnamed x9, local copies, waits for them, and re-layouts  3.38 us

profile of v1, /device:TPU:0, one launch (start us, length us, event | category | flops | bytes accessed | tf_op | source)
XLA Modules:
  0.0 40.1 jit_solution(11946892763657076515)
XLA Ops:
  0.0 0.8 %copy.7.in_pat = s32[8,1,2]{2,1,0:T(1,128)S(1)} copy(s32[8,1,2]{0,2,1:T(2,128)} %param.6) | data formatting | bytes 128 | tf_op args[1]
  0.8 0.0 copy-start
  0.8 0.0 copy-start.1
  0.8 0.0 copy-start.2
  0.8 1.9 %copy.6.panel = bf16[1024,1,256]{2,1,0:T(2,128)(2,1)S(1)} copy(bf16[1024,1,256]{2,0,1:T(8,128)(2,1)} %param.5) | data formatting | bytes 1048576 | tf_op args[0]
  2.7 0.0 copy-done
  2.7 0.0 copy-done.1
  2.7 0.0 copy-done.2
  2.7 36.7 %shard_map.55 = bf16[256,512]{1,0:T(8,128)(2,1)S(1)} custom-call(bf16[1024,1,256]{2,1,0:T(2,128)(2,1)S(1)} %copy.6.panel, s32[8,1,2]{2,1,0:T(1,128)S(1)} %copy.7.in_pat, bf16[1,4,128,512]{3,2,1,0:T(8,128)(2,1)S(1)} %copy-done, s32[1,8]{1,0:T(1,128)S(1)} %copy-done.2, s32[2,4]{1,0:T(2,128)S(1)} %copy-done.1), custom_call_target="tpu_custom_call" | custom-call | tf_op jit(solution)/shard_map/pallas_call | solution.py:226
  39.4 0.7 %copy.9 = bf16[256,512]{1,0:T(8,128)(2,1)} copy(bf16[256,512]{1,0:T(8,128)(2,1)S(1)} %shard_map.55) | data formatting | bytes 524288
Async XLA Ops:
  0.8 1.9 %copy-start = (bf16[1,4,128,512]{3,2,1,0:T(8,128)(2,1)S(1)}, bf16[1,4,128,512]{3,2,1,0:T(8,128)(2,1)}, u32[]{:S(2)}) copy-start(bf16[1,4,128,512]{3,2,1,0:T(8,128)(2,1)} %slab.1) | copy-start | bytes 1572868
  0.8 1.9 %copy-start.1 = (s32[2,4]{1,0:T(2,128)S(1)}, s32[2,4]{1,0:T(2,128)}, u32[]{:S(2)}) copy-start(s32[2,4]{1,0:T(2,128)} %out_pat.1) | copy-start | bytes 100
  0.8 1.9 %copy-start.2 = (s32[1,8]{1,0:T(1,128)S(1)}, s32[1,8]{1,0:T(1,128)}, u32[]{:S(2)}) copy-start(s32[1,8]{1,0:T(1,128)} %owner.1) | copy-start | bytes 100

commit v2 on v1

--- a/solution.py
+++ b/solution.py
@@ -40,7 +40,7 @@
     mate = half * 2 + (1 - side)
     rows = out.shape[0]
     bs = slab.shape[2]
-    depth = panel.shape[2]
+    depth = panel.shape[1]
     wide = out.shape[1] // N
     mine = slab.shape[1]
     brows = rows // bs
@@ -76,8 +76,8 @@
         for i in range(brows):
             first = pl.multiple_of(dest[t] * rows + i * bs, bs)
             for j in range(depth // bs):
-                keep = in_pat[dest[t] * brows + i, 0, j].astype(jnp.float32)
-                block = panel[pl.ds(first, bs), 0, j * bs : (j + 1) * bs].astype(jnp.float32)
+                keep = in_pat[j, dest[t] * brows + i].astype(jnp.float32)
+                block = panel[pl.ds(first, bs), j * bs : (j + 1) * bs].astype(jnp.float32)
                 portion[col, t, i * bs : (i + 1) * bs, j * bs : (j + 1) * bs] = (block * keep).astype(jnp.bfloat16)
 
     def send_part(c_to, t, sem):
@@ -106,13 +106,13 @@
 
     mask(0)
     pl.semaphore_wait(barrier, (R - 1) + H + jnp.where(z > 0, 1, 0) + jnp.where(z < L - 1, 1, 0))
-    start_slab(0)
-    start_parts(0)
-    for t in range(1, L):
-        mask(t)
-        start_parts(t)
-    for n in range(1, N):
-        start_slab(n)
+    for t in range(max(L, N)):
+        if t < N:
+            start_slab(t)
+        if t < L:
+            if t > 0:
+                mask(t)
+            start_parts(t)
     for n in range(N):
         slabs[n][pl.ds(row * mine, mine)] = slab[0, :, :, n * wide : (n + 1) * wide]
 
@@ -152,15 +152,15 @@
         up = jnp.where(dest[t] > z, 1, 0)
         return dest[t] + L * (1 - up), z + 2 * up - 1
 
-    for n in range(N):
-        for t in range(L - 1):
-            if n == 0:
-                ready_parts(t)
-                if t == 0:
-                    ready_slab(0)
-                wait_parts(t)
-            elif t == 0:
-                ready_slab(n)
+    for stage in range(max(L - 1, N)):
+        if stage < L - 1:
+            ready_parts(stage)
+        if stage < N:
+            ready_slab(stage)
+        if stage < L - 1:
+            wait_parts(stage)
+        pieces = [(t, n) for t in range(L - 1) for n in range(N) if max(t, n) == stage]
+        for t, n in sorted(pieces, key=lambda piece: (sum(piece), piece)):
             slot, to = route(t)
             inner = (z > 0) & (z < L - 1)
 
@@ -211,7 +211,7 @@
 
 def solution(mesh):
     R, C, L = (mesh.shape[name] for name in ("row", "col", "layer"))
-    N = 2
+    N = 4
 
     def shards(panel, in_pat, slab, owner, out_pat):
         bs, cols = slab.shape[2], slab.shape[3]
@@ -246,7 +246,7 @@
             ],
             compiler_params=pltpu.CompilerParams(
                 collective_id=0, has_side_effects=True, vmem_limit_bytes=48 * 2**20),
-        )(panel, in_pat, slab, owner, out_pat)
+        )(panel.reshape(panel.shape[0], depth), in_pat[:, 0, :].T, slab, owner, out_pat)
 
     in_specs = (
         P("row", "layer", "col"),

time: 40.3 us -> 41.6 us (1.032)
  Pallas kernels: 36.7 us -> 37.9 us
    pallas_call x1, Pallas kernels: 36.7 us -> 37.9 us  [shards(): pl.pallas_call(functools.partial(kernel, (R, C, L, N)), out_shape=jax.Sha...]
    unnamed x9 -> x11, local copies, waits for them, and re-layouts: 3.38 us -> 3.48 us
where the time goes in v2:
time: 41.6 us; the launch traced here: 41.4 us
  Pallas kernels  37.9 us (91%)
  local copies, waits for them, and re-layouts  3.48 us (8%)
    pallas_call x1, Pallas kernels, shards(): pl.pallas_call(functools.partial(kernel, (R, C, L, N)), out_shape=jax.Sha...  37.9 us
    unnamed x11, local copies, waits for them, and re-layouts  3.48 us

profile of v2, /device:TPU:0, one launch (start us, length us, event | category | flops | bytes accessed | tf_op | source)
XLA Modules:
  0.0 41.4 jit_solution(15091096463290415343)
XLA Ops:
  0.0 0.0 copy-start.3
  0.0 0.0 copy-start.2
  0.0 0.0 copy-start.4
  0.0 0.7 %copy-done.3 = s32[2,4]{1,0:T(2,128)S(1)} copy-done((s32[2,4]{1,0:T(2,128)S(1)}, s32[2,4]{1,0:T(2,128)}, u32[]{:S(2)}) %copy-start.3) | copy-done | bytes 56
  0.7 0.0 copy-done.2
  0.7 0.0 copy-done.4
  0.7 0.0 copy-start
  0.7 1.0 %copy-done = bf16[1024,1,256]{2,0,1:T(8,128)(2,1)S(1)} copy-done((bf16[1024,1,256]{2,0,1:T(8,128)(2,1)S(1)}, bf16[1024,1,256]{2,0,1:T(8,128)(2,1)}, u32[]{:S(2)}) %copy-start) | copy-done | bytes 524312
  1.7 0.0 copy-start.1
  1.7 1.0 %copy-done.1 = bf16[1,4,128,512]{3,2,1,0:T(8,128)(2,1)S(1)} copy-done((bf16[1,4,128,512]{3,2,1,0:T(8,128)(2,1)S(1)}, bf16[1,4,128,512]{3,2,1,0:T(8,128)(2,1)}, u32[]{:S(2)}) %copy-start.1) | copy-done | bytes 524312
  2.8 37.9 %shard_map.55 = bf16[256,512]{1,0:T(8,128)(2,1)S(1)} custom-call(bf16[1024,256]{1,0:T(8,128)(2,1)S(1)} %bitcast.4, s32[2,8]{1,0:T(2,128)S(1)} %bitcast.5, bf16[1,4,128,512]{3,2,1,0:T(8,128)(2,1)S(1)} %copy-done.1, s32[1,8]{1,0:T(1,128)S(1)} %copy-done.4, s32[2,4]{1,0:T(2,128)S(1)} %copy-done.3), custom_call_target="tpu_custom_call" | custom-call | tf_op jit(solution)/shard_map/pallas_call | solution.py:226
  40.7 0.7 %copy.7 = bf16[256,512]{1,0:T(8,128)(2,1)} copy(bf16[256,512]{1,0:T(8,128)(2,1)S(1)} %shard_map.55) | data formatting | bytes 524288
Async XLA Ops:
  0.0 0.7 %copy-start.3 = (s32[2,4]{1,0:T(2,128)S(1)}, s32[2,4]{1,0:T(2,128)}, u32[]{:S(2)}) copy-start(s32[2,4]{1,0:T(2,128)} %out_pat.1) | copy-start | bytes 100
  0.0 0.7 %copy-start.2 = (s32[8,1,2]{0,2,1:T(2,128)S(1)}, s32[8,1,2]{0,2,1:T(2,128)}, u32[]{:S(2)}) copy-start(s32[8,1,2]{0,2,1:T(2,128)} %param.6) | copy-start | bytes 196
  0.0 0.7 %copy-start.4 = (s32[1,8]{1,0:T(1,128)S(1)}, s32[1,8]{1,0:T(1,128)}, u32[]{:S(2)}) copy-start(s32[1,8]{1,0:T(1,128)} %owner.1) | copy-start | bytes 100
  0.7 1.0 %copy-start = (bf16[1024,1,256]{2,0,1:T(8,128)(2,1)S(1)}, bf16[1024,1,256]{2,0,1:T(8,128)(2,1)}, u32[]{:S(2)}) copy-start(bf16[1024,1,256]{2,0,1:T(8,128)(2,1)} %param.5) | copy-start | bytes 1572868
  1.7 1.0 %copy-start.1 = (bf16[1,4,128,512]{3,2,1,0:T(8,128)(2,1)S(1)}, bf16[1,4,128,512]{3,2,1,0:T(8,128)(2,1)}, u32[]{:S(2)}) copy-start(bf16[1,4,128,512]{3,2,1,0:T(8,128)(2,1)} %slab.1) | copy-start | bytes 1572868

commit v3 on v2

--- a/solution.py
+++ b/solution.py
@@ -30,19 +30,20 @@
     return message[0:rows, :].astype(jnp.int32).astype(jnp.float32) * factor
 
 
-def kernel(sizes, panel, in_pat, slab, owner, out_pat, out, *scratch):
-    R, C, L, N = sizes
-    slabs, ops = scratch[:N], scratch[N : 2 * N]
-    portion, sbuf, rbuf, acc, sx, sc, sr, rp, ss, rs, sz, rz = scratch[2 * N :]
+def kernel(sizes, widths, panel_hbm, in_hbm, slab_hbm, owner_hbm, out_hbm, out, *scratch):
+    R, C, L = sizes
+    N = len(widths)
+    starts = [sum(widths[:n]) for n in range(N)]
+    slabs, ops, sbufs, rbufs = (scratch[i * N : (i + 1) * N] for i in range(4))
+    panel, in_pat, owner, out_pat, portion, acc, lp, ls, lm, sx, sc, sr, rp, ss, rs, sz, rz = scratch[4 * N :]
     H = C // 2
     row, col, z = lax.axis_index("row"), lax.axis_index("col"), lax.axis_index("layer")
     half, side = col // 2, col % 2
     mate = half * 2 + (1 - side)
     rows = out.shape[0]
-    bs = slab.shape[2]
+    bs = slab_hbm.shape[2]
     depth = panel.shape[1]
-    wide = out.shape[1] // N
-    mine = slab.shape[1]
+    mine = slab_hbm.shape[1]
     brows = rows // bs
     hops = [((half + i) % H) * 2 + side for i in range(1, H)]
     relays = [((half + i) % H) * 2 + (1 - side) for i in range(1, H)]
@@ -71,6 +72,29 @@
         return found
 
     dest = [pick(t) for t in range(L)]
+
+    def load_panel(t):
+        here = pl.ds(pl.multiple_of(dest[t] * rows, rows), rows)
+        return pltpu.make_async_copy(panel_hbm.at[here], panel.at[here], lp.at[t])
+
+    def load_slab(n):
+        return pltpu.make_async_copy(
+            slab_hbm.at[0, :, :, pl.ds(starts[n], widths[n])], slabs[n].at[pl.ds(row * mine, mine)], ls.at[n])
+
+    small = [
+        pltpu.make_async_copy(src, dst, lm.at[i])
+        for i, (src, dst) in enumerate([(in_hbm, in_pat), (owner_hbm, owner), (out_hbm, out_pat)])
+    ]
+    small[0].start()
+    load_panel(0).start()
+    load_slab(0).start()
+    for t in range(1, max(L, N)):
+        if t < L:
+            load_panel(t).start()
+        if t < N:
+            load_slab(t).start()
+    small[1].start()
+    small[2].start()
 
     def mask(t):
         for i in range(brows):
@@ -91,9 +115,10 @@
             device_id={"col": mate}, device_id_type=MESH)
 
     def send_slab(r_to, i, n):
+        block = slabs[n].at[pl.ds(row * mine, mine)]
         return pltpu.make_async_remote_copy(
-            src_ref=slab.at[0, :, :, pl.ds(n * wide, wide)], dst_ref=slabs[n].at[pl.ds(row * mine, mine)],
-            send_sem=ss.at[i, n], recv_sem=rs.at[row, n], device_id={"row": r_to}, device_id_type=MESH)
+            src_ref=block, dst_ref=block, send_sem=ss.at[i, n], recv_sem=rs.at[row, n],
+            device_id={"row": r_to}, device_id_type=MESH)
 
     def start_parts(t):
         for i, c in enumerate(hops):
@@ -104,17 +129,23 @@
         for i, r in enumerate(peers):
             send_slab(r, i, n).start()
 
+    small[0].wait()
+    load_panel(0).wait()
     mask(0)
+    load_slab(0).wait()
     pl.semaphore_wait(barrier, (R - 1) + H + jnp.where(z > 0, 1, 0) + jnp.where(z < L - 1, 1, 0))
-    for t in range(max(L, N)):
+    start_slab(0)
+    start_parts(0)
+    for t in range(1, max(L, N)):
         if t < N:
+            load_slab(t).wait()
             start_slab(t)
         if t < L:
-            if t > 0:
-                mask(t)
+            load_panel(t).wait()
+            mask(t)
             start_parts(t)
-    for n in range(N):
-        slabs[n][pl.ds(row * mine, mine)] = slab[0, :, :, n * wide : (n + 1) * wide]
+    small[1].wait()
+    small[2].wait()
 
     def ready_parts(t):
         for i, c in enumerate(hops):
@@ -141,46 +172,55 @@
 
     def message(t, n, slot, to):
         return pltpu.make_async_remote_copy(
-            src_ref=sbuf.at[t, n], dst_ref=rbuf.at[slot, n], send_sem=sz.at[t, n], recv_sem=rz.at[slot, n],
+            src_ref=sbufs[n].at[t], dst_ref=rbufs[n].at[slot], send_sem=sz.at[t, n], recv_sem=rz.at[slot, n],
             device_id={"layer": to}, device_id_type=MESH)
 
     def arrived(slot, n):
         message(0, n, slot, (z + 1) % L).wait_recv()
-        return decode(rbuf.at[slot, n], rows)
+        return decode(rbufs[n].at[slot], rows)
 
     def route(t):
         up = jnp.where(dest[t] > z, 1, 0)
         return dest[t] + L * (1 - up), z + 2 * up - 1
 
+    inner = (z > 0) & (z < L - 1)
+
+    def pass_on(t, n):
+        slot, to = route(t)
+
+        @pl.when(inner)
+        def _():
+            total = product(t, n)
+            encode(total + arrived(slot, n), sbufs[n].at[t])
+
+        @pl.when(jnp.logical_not(inner))
+        def _():
+            encode(product(t, n), sbufs[n].at[t])
+
+        message(t, n, slot, to).start()
+
     for stage in range(max(L - 1, N)):
+        last = stage == max(L - 1, N) - 1
         if stage < L - 1:
             ready_parts(stage)
+            if stage == 0:
+                ready_slab(0)
+            wait_parts(stage)
+            for n in range(min(stage, N)):
+                pass_on(stage, n)
+        if 0 < stage < N:
+            ready_slab(stage)
         if stage < N:
-            ready_slab(stage)
-        if stage < L - 1:
-            wait_parts(stage)
-        pieces = [(t, n) for t in range(L - 1) for n in range(N) if max(t, n) == stage]
-        for t, n in sorted(pieces, key=lambda piece: (sum(piece), piece)):
-            slot, to = route(t)
-            inner = (z > 0) & (z < L - 1)
-
-            @pl.when(inner)
-            def _(t=t, n=n, slot=slot):
-                total = product(t, n)
-                encode(total + arrived(slot, n), sbuf.at[t, n])
-
-            @pl.when(jnp.logical_not(inner))
-            def _(t=t, n=n):
-                encode(product(t, n), sbuf.at[t, n])
-
-            message(t, n, slot, to).start()
-
-    ready_parts(L - 1)
-    wait_parts(L - 1)
+            for t in range(min(stage + 1, L - 1)):
+                pass_on(t, stage)
+                if last and t == 0:
+                    ready_parts(L - 1)
+                    wait_parts(L - 1)
+                    for n in range(N):
+                        acc[:, starts[n] : starts[n] + widths[n]] = product(L - 1, n)
+
     for n in range(N):
-        acc[:, n * wide : (n + 1) * wide] = product(L - 1, n)
-    for n in range(N):
-        here = slice(n * wide, (n + 1) * wide)
+        here = slice(starts[n], starts[n] + widths[n])
 
         @pl.when(z > 0)
         def _():
@@ -191,7 +231,7 @@
             acc[:, here] += arrived(z + L, n)
 
         for i in range(brows):
-            for j in range(n * wide // bs, (n + 1) * wide // bs):
+            for j in range(starts[n] // bs, (starts[n] + widths[n]) // bs):
                 keep = out_pat[i, j].astype(jnp.float32)
                 at = (slice(i * bs, (i + 1) * bs), slice(j * bs, (j + 1) * bs))
                 out[at] = (acc[at] * keep).astype(jnp.bfloat16)
@@ -211,30 +251,37 @@
 
 def solution(mesh):
     R, C, L = (mesh.shape[name] for name in ("row", "col", "layer"))
-    N = 4
 
     def shards(panel, in_pat, slab, owner, out_pat):
         bs, cols = slab.shape[2], slab.shape[3]
         rows = panel.shape[0] // L
         depth = panel.shape[2]
         blocks = R * slab.shape[1]
-        wide = cols // N
+        widths = (cols // 4, cols // 4, cols // 2)
+        N = len(widths)
         H = C // 2
         dma = pltpu.SemaphoreType.DMA
         vmem = pl.BlockSpec(memory_space=pltpu.VMEM)
-        smem = pl.BlockSpec(memory_space=pltpu.SMEM)
+        hbm = pl.BlockSpec(memory_space=pl.ANY)
         return pl.pallas_call(
-            functools.partial(kernel, (R, C, L, N)),
+            functools.partial(kernel, (R, C, L), widths),
             out_shape=jax.ShapeDtypeStruct((rows, cols), jnp.bfloat16),
-            in_specs=[vmem, smem, vmem, smem, smem],
+            in_specs=[hbm] * 5,
             out_specs=vmem,
-            scratch_shapes=[pltpu.VMEM((blocks, bs, wide), jnp.bfloat16) for _ in range(N)]
-            + [pltpu.VMEM((blocks * bs, wide), jnp.bfloat16) for _ in range(N)]
+            scratch_shapes=[pltpu.VMEM((blocks, bs, w), jnp.bfloat16) for w in widths]
+            + [pltpu.VMEM((blocks * bs, w), jnp.bfloat16) for w in widths]
+            + [pltpu.VMEM((L - 1, rows + PAD, w), jnp.int16) for w in widths]
+            + [pltpu.VMEM((2 * L, rows + PAD, w), jnp.int16) for w in widths]
             + [
+                pltpu.VMEM((panel.shape[0], depth), jnp.bfloat16),
+                pltpu.SMEM((in_pat.shape[2], in_pat.shape[0]), jnp.int32),
+                pltpu.SMEM(owner.shape, jnp.int32),
+                pltpu.SMEM(out_pat.shape, jnp.int32),
                 pltpu.VMEM((C, L, rows, depth), jnp.bfloat16),
-                pltpu.VMEM((L - 1, N, rows + PAD, wide), jnp.int16),
-                pltpu.VMEM((2 * L, N, rows + PAD, wide), jnp.int16),
                 pltpu.VMEM((rows, cols), jnp.float32),
+                dma((L,)),
+                dma((N,)),
+                dma((3,)),
                 dma((H - 1, L)),
                 dma((L,)),
                 dma((H - 1, L)),
@@ -245,7 +292,7 @@
                 dma((2 * L, N)),
             ],
             compiler_params=pltpu.CompilerParams(
-                collective_id=0, has_side_effects=True, vmem_limit_bytes=48 * 2**20),
+                collective_id=0, has_side_effects=True, vmem_limit_bytes=56 * 2**20),
         )(panel.reshape(panel.shape[0], depth), in_pat[:, 0, :].T, slab, owner, out_pat)
 
     in_specs = (

time: 41.6 us -> 39.8 us (0.957)
  local copies, waits for them, and re-layouts: 3.48 us -> 1.67 us
    unnamed x11 -> x1, local copies, waits for them, and re-layouts: 3.48 us -> 1.67 us
where the time goes in v3:
time: 39.8 us; the launch traced here: 39.6 us
  Pallas kernels  37.9 us (95%)
  local copies, waits for them, and re-layouts  1.67 us (4%)
    pallas_call x1, Pallas kernels, shards(): pl.pallas_call(functools.partial(kernel, (R, C, L), widths), out_shape=ja...  37.9 us
    unnamed x1, local copies, waits for them, and re-layouts  1.67 us

profile of v3, /device:TPU:0, one launch (start us, length us, event | category | flops | bytes accessed | tf_op | source)
XLA Modules:
  0.0 39.6 jit_solution(14917065789289724616)
XLA Ops:
  0.0 37.9 %shard_map.55 = bf16[256,512]{1,0:T(8,128)(2,1)} custom-call(bf16[1024,256]{1,0:T(8,128)(2,1)} %bitcast.4, s32[2,8]{1,0:T(2,128)} %bitcast.5, bf16[1,4,128,512]{3,2,1,0:T(8,128)(2,1)} %slab_hbm.1, s32[1,8]{1,0:T(1,128)} %owner_hbm.1, s32[2,4]{1,0:T(2,128)} %out_hbm.1), custom_call_target="tpu_custom_call" | custom-call | tf_op jit(solution)/shard_map/pallas_call | solution.py:266
  38.0 1.7 %copy.7 = bf16[256,512]{1,0:T(8,128)(2,1)} copy(bf16[256,512]{1,0:T(8,128)(2,1)} %shard_map.55) | data formatting | bytes 524288

commit v4 on v3

--- a/solution.py
+++ b/solution.py
@@ -63,7 +63,7 @@
     def _():
         pl.semaphore_signal(barrier, inc=1, device_id={"layer": z + 1}, device_id_type=MESH)
 
-    tables = [sorted(range(L), key=lambda d: (-abs(d - i), d)) for i in range(L)]
+    tables = [sorted(range(L), key=lambda d: (-abs(d - i), -i if d > i else i - L + 1)) for i in range(L)]
 
     def pick(t):
         found = 0
@@ -165,10 +165,8 @@
             ops[n][j * bs : (j + 1) * bs, :] = slabs[n][owner[0, j]]
 
     def product(t, n):
-        total = jnp.dot(portion[0, t], ops[n][0:depth, :], preferred_element_type=jnp.float32)
-        for c in range(1, C):
-            total += jnp.dot(portion[c, t], ops[n][c * depth : (c + 1) * depth, :], preferred_element_type=jnp.float32)
-        return total
+        left = jnp.concatenate([portion[c, t] for c in range(C)], axis=1)
+        return jnp.dot(left, ops[n][...], preferred_element_type=jnp.float32)
 
     def message(t, n, slot, to):
         return pltpu.make_async_remote_copy(
@@ -199,25 +197,29 @@
 
         message(t, n, slot, to).start()
 
-    for stage in range(max(L - 1, N)):
-        last = stage == max(L - 1, N) - 1
-        if stage < L - 1:
-            ready_parts(stage)
-            if stage == 0:
-                ready_slab(0)
-            wait_parts(stage)
-            for n in range(min(stage, N)):
-                pass_on(stage, n)
-        if 0 < stage < N:
-            ready_slab(stage)
-        if stage < N:
-            for t in range(min(stage + 1, L - 1)):
-                pass_on(t, stage)
-                if last and t == 0:
-                    ready_parts(L - 1)
-                    wait_parts(L - 1)
-                    for n in range(N):
-                        acc[:, starts[n] : starts[n] + widths[n]] = product(L - 1, n)
+    ready_parts(0)
+    ready_slab(0)
+    wait_parts(0)
+    pass_on(0, 0)
+    for n in range(1, N):
+        ready_slab(n)
+        pass_on(0, n)
+        if n == 1 and L > 2:
+            ready_parts(1)
+            wait_parts(1)
+            pass_on(1, 0)
+        if n == N - 1:
+            for t in range(min(2, L - 1), L):
+                ready_parts(t)
+            for t in range(min(2, L - 1), L):
+                wait_parts(t)
+            for m in range(N):
+                acc[:, starts[m] : starts[m] + widths[m]] = product(L - 1, m)
+        if L > 2:
+            pass_on(1, n)
+    for t in range(2, L - 1):
+        for n in range(N):
+            pass_on(t, n)
 
     for n in range(N):
         here = slice(starts[n], starts[n] + widths[n])
@@ -257,12 +259,12 @@
         rows = panel.shape[0] // L
         depth = panel.shape[2]
         blocks = R * slab.shape[1]
-        widths = (cols // 4, cols // 4, cols // 2)
+        widths = (cols // 4,) * 4
         N = len(widths)
         H = C // 2
         dma = pltpu.SemaphoreType.DMA
         vmem = pl.BlockSpec(memory_space=pltpu.VMEM)
-        hbm = pl.BlockSpec(memory_space=pl.ANY)
+        hbm = pl.BlockSpec(memory_space=pltpu.HBM)
         return pl.pallas_call(
             functools.partial(kernel, (R, C, L), widths),
             out_shape=jax.ShapeDtypeStruct((rows, cols), jnp.bfloat16),

time: 39.8 us -> 39.2 us (0.985)
  the two profiles are of different devices: /device:TPU:0 before, /device:TPU:8 now
where the time goes in v4:
time: 39.2 us; the launch traced here: 39.1 us
  Pallas kernels  37.4 us (95%)
  local copies, waits for them, and re-layouts  1.67 us (4%)
    pallas_call x1, Pallas kernels, shards(): pl.pallas_call(functools.partial(kernel, (R, C, L), widths), out_shape=ja...  37.4 us
    unnamed x1, local copies, waits for them, and re-layouts  1.67 us

profile of v4, /device:TPU:8, one launch (start us, length us, event | category | flops | bytes accessed | tf_op | source)
XLA Modules:
  0.0 39.1 jit_solution(6550168907016514831)
XLA Ops:
  0.0 37.4 %shard_map.55 = bf16[256,512]{1,0:T(8,128)(2,1)} custom-call(bf16[1024,256]{1,0:T(8,128)(2,1)} %bitcast.4, s32[2,8]{1,0:T(2,128)} %bitcast.5, bf16[1,4,128,512]{3,2,1,0:T(8,128)(2,1)} %slab_hbm.1, s32[1,8]{1,0:T(1,128)} %owner_hbm.1, s32[2,4]{1,0:T(2,128)} %out_hbm.1), custom_call_target="tpu_custom_call" | custom-call | tf_op jit(solution)/shard_map/pallas_call | solution.py:268
  37.4 1.7 %copy.7 = bf16[256,512]{1,0:T(8,128)(2,1)} copy(bf16[256,512]{1,0:T(8,128)(2,1)} %shard_map.55) | data formatting | bytes 524288

commit v5 on v4

--- a/solution.py
+++ b/solution.py
@@ -34,8 +34,8 @@
     R, C, L = sizes
     N = len(widths)
     starts = [sum(widths[:n]) for n in range(N)]
-    slabs, ops, sbufs, rbufs = (scratch[i * N : (i + 1) * N] for i in range(4))
-    panel, in_pat, owner, out_pat, portion, acc, lp, ls, lm, sx, sc, sr, rp, ss, rs, sz, rz = scratch[4 * N :]
+    slabs, sbufs, rbufs = (scratch[i * N : (i + 1) * N] for i in range(3))
+    ops, panel, in_pat, owner, out_pat, portion, acc, lp, ls, lm, sx, sc, sr, rp, ss, rs, sz, rz = scratch[3 * N :]
     H = C // 2
     row, col, z = lax.axis_index("row"), lax.axis_index("col"), lax.axis_index("layer")
     half, side = col // 2, col % 2
@@ -162,11 +162,17 @@
                 src_ref=slabs[n].at[pl.ds(r * mine, mine)], dst_ref=slabs[n].at[pl.ds(r * mine, mine)],
                 send_sem=ss.at[0, n], recv_sem=rs.at[r, n], device_id={"row": r}, device_id_type=MESH).wait_recv()
         for j in range(R * mine):
-            ops[n][j * bs : (j + 1) * bs, :] = slabs[n][owner[0, j]]
+            ops[j * bs : (j + 1) * bs, starts[n] : starts[n] + widths[n]] = slabs[n][owner[0, j]]
+
+    near = min(2, L - 1)
 
     def product(t, n):
         left = jnp.concatenate([portion[c, t] for c in range(C)], axis=1)
-        return jnp.dot(left, ops[n][...], preferred_element_type=jnp.float32)
+        return jnp.dot(left, ops[:, starts[n] : starts[n] + widths[n]], preferred_element_type=jnp.float32)
+
+    def multiply_near():
+        left = [portion[c, near:L].reshape((L - near) * rows, depth) for c in range(C)]
+        acc[...] = jnp.dot(jnp.concatenate(left, axis=1), ops[...], preferred_element_type=jnp.float32)
 
     def message(t, n, slot, to):
         return pltpu.make_async_remote_copy(
@@ -183,60 +189,98 @@
 
     inner = (z > 0) & (z < L - 1)
 
-    def pass_on(t, n):
+    def pass_on(t, n, add):
         slot, to = route(t)
+        if t < near:
+            total = product(t, n)
+        else:
+            total = acc[(t - near) * rows : (t - near + 1) * rows, starts[n] : starts[n] + widths[n]]
+        if add:
+            total = total + arrived(slot, n)
+        encode(total, sbufs[n].at[t])
+        message(t, n, slot, to).start()
+
+    def parts(*steps):
+        for t in steps:
+            ready_parts(t)
+        for t in steps:
+            wait_parts(t)
+
+    def finish(n, up, down):
+        here = slice(starts[n], starts[n] + widths[n])
+        total = acc[(L - 1 - near) * rows :, here]
+        if up:
+            total = total + arrived(z, n)
+        if down:
+            total = total + arrived(z + L, n)
+        for i in range(brows):
+            for j in range(widths[n] // bs):
+                keep = out_pat[i, starts[n] // bs + j].astype(jnp.float32)
+                block = total[i * bs : (i + 1) * bs, j * bs : (j + 1) * bs] * keep
+                first = starts[n] + j * bs
+                out[i * bs : (i + 1) * bs, first : first + bs] = block.astype(jnp.bfloat16)
+
+    late = list(range(near, L))
+    tail = [(t, n) for t in range(2, L - 1) for n in range(N)]
+
+    @pl.when(jnp.logical_not(inner))
+    def _():
+        for n in range(N):
+            if n == 0:
+                ready_parts(0)
+            ready_slab(n)
+            if n == 0:
+                wait_parts(0)
+            pass_on(0, n, False)
+            if n == 1 and near > 1:
+                parts(1)
+                pass_on(1, 0, False)
+            if n > 0 and near > 1:
+                pass_on(1, n, False)
+        parts(*late)
+        multiply_near()
+        for t, n in tail:
+            pass_on(t, n, False)
+
+        @pl.when(z > 0)
+        def _():
+            for n in range(N):
+                finish(n, True, False)
+
+        @pl.when(z == 0)
+        def _():
+            for n in range(N):
+                finish(n, False, L > 1)
+
+    if L > 2:
 
         @pl.when(inner)
         def _():
-            total = product(t, n)
-            encode(total + arrived(slot, n), sbufs[n].at[t])
-
-        @pl.when(jnp.logical_not(inner))
-        def _():
-            encode(product(t, n), sbufs[n].at[t])
-
-        message(t, n, slot, to).start()
-
-    ready_parts(0)
-    ready_slab(0)
-    wait_parts(0)
-    pass_on(0, 0)
-    for n in range(1, N):
-        ready_slab(n)
-        pass_on(0, n)
-        if n == 1 and L > 2:
-            ready_parts(1)
-            wait_parts(1)
-            pass_on(1, 0)
-        if n == N - 1:
-            for t in range(min(2, L - 1), L):
-                ready_parts(t)
-            for t in range(min(2, L - 1), L):
-                wait_parts(t)
-            for m in range(N):
-                acc[:, starts[m] : starts[m] + widths[m]] = product(L - 1, m)
-        if L > 2:
-            pass_on(1, n)
-    for t in range(2, L - 1):
-        for n in range(N):
-            pass_on(t, n)
-
-    for n in range(N):
-        here = slice(starts[n], starts[n] + widths[n])
-
-        @pl.when(z > 0)
-        def _():
-            acc[:, here] += arrived(z, n)
-
-        @pl.when(z < L - 1)
-        def _():
-            acc[:, here] += arrived(z + L, n)
-
-        for i in range(brows):
-            for j in range(starts[n] // bs, (starts[n] + widths[n]) // bs):
-                keep = out_pat[i, j].astype(jnp.float32)
-                at = (slice(i * bs, (i + 1) * bs), slice(j * bs, (j + 1) * bs))
-                out[at] = (acc[at] * keep).astype(jnp.bfloat16)
+            for n in range(N):
+                if n == 0:
+                    ready_parts(0)
+                ready_slab(n)
+                if n == 0:
+                    wait_parts(0)
+                if n == N - 1:
+                    parts(*late)
+                    multiply_near()
+                    if N > 2:
+                        pass_on(1, N - 3, True)
+                pass_on(0, n, True)
+                if n == 0:
+                    parts(1)
+                elif n < N - 1 and n > 1:
+                    pass_on(1, n - 2, True)
+            order = [(1, n) for n in range(max(N - 2, 0), N)]
+            for i, (t, n) in enumerate(tail):
+                if i < len(order):
+                    pass_on(*order[i], True)
+                pass_on(t, n, True)
+            for t, n in order[len(tail) :]:
+                pass_on(t, n, True)
+            for n in range(N):
+                finish(n, True, True)
 
     for t in range(L):
         for i, c in enumerate(hops):
@@ -271,16 +315,16 @@
             in_specs=[hbm] * 5,
             out_specs=vmem,
             scratch_shapes=[pltpu.VMEM((blocks, bs, w), jnp.bfloat16) for w in widths]
-            + [pltpu.VMEM((blocks * bs, w), jnp.bfloat16) for w in widths]
             + [pltpu.VMEM((L - 1, rows + PAD, w), jnp.int16) for w in widths]
             + [pltpu.VMEM((2 * L, rows + PAD, w), jnp.int16) for w in widths]
             + [
+                pltpu.VMEM((blocks * bs, cols), jnp.bfloat16),
                 pltpu.VMEM((panel.shape[0], depth), jnp.bfloat16),
                 pltpu.SMEM((in_pat.shape[2], in_pat.shape[0]), jnp.int32),
                 pltpu.SMEM(owner.shape, jnp.int32),
                 pltpu.SMEM(out_pat.shape, jnp.int32),
                 pltpu.VMEM((C, L, rows, depth), jnp.bfloat16),
-                pltpu.VMEM((rows, cols), jnp.float32),
+                pltpu.VMEM(((L - min(2, L - 1)) * rows, cols), jnp.float32),
                 dma((L,)),
                 dma((N,)),
                 dma((3,)),

time: 39.2 us -> 36.2 us (0.923)
  the two profiles are of different devices: /device:TPU:8 before, /device:TPU:0 now
where the time goes in v5:
time: 36.2 us; the launch traced here: 36 us
  Pallas kernels  34.3 us (95%)
  local copies, waits for them, and re-layouts  1.67 us (5%)
    pallas_call x1, Pallas kernels, shards(): pl.pallas_call(functools.partial(kernel, (R, C, L), widths), out_shape=ja...  34.3 us
    unnamed x1, local copies, waits for them, and re-layouts  1.67 us

profile of v5, /device:TPU:0, one launch (start us, length us, event | category | flops | bytes accessed | tf_op | source)
XLA Modules:
  0.0 36.0 jit_solution(4076669505043241225)
XLA Ops:
  0.0 34.3 %shard_map.55 = bf16[256,512]{1,0:T(8,128)(2,1)} custom-call(bf16[1024,256]{1,0:T(8,128)(2,1)} %bitcast.4, s32[2,8]{1,0:T(2,128)} %bitcast.5, bf16[1,4,128,512]{3,2,1,0:T(8,128)(2,1)} %slab_hbm.1, s32[1,8]{1,0:T(1,128)} %owner_hbm.1, s32[2,4]{1,0:T(2,128)} %out_hbm.1), custom_call_target="tpu_custom_call" | custom-call | tf_op jit(solution)/shard_map/pallas_call | solution.py:312
  34.4 1.7 %copy.7 = bf16[256,512]{1,0:T(8,128)(2,1)} copy(bf16[256,512]{1,0:T(8,128)(2,1)} %shard_map.55) | data formatting | bytes 524288

commit v6 on v5

--- a/solution.py
+++ b/solution.py
@@ -170,9 +170,9 @@
         left = jnp.concatenate([portion[c, t] for c in range(C)], axis=1)
         return jnp.dot(left, ops[:, starts[n] : starts[n] + widths[n]], preferred_element_type=jnp.float32)
 
-    def multiply_near():
-        left = [portion[c, near:L].reshape((L - near) * rows, depth) for c in range(C)]
-        acc[...] = jnp.dot(jnp.concatenate(left, axis=1), ops[...], preferred_element_type=jnp.float32)
+    def multiply_from(t):
+        left = [portion[c, t:L].reshape((L - t) * rows, depth) for c in range(C)]
+        acc[(t - near) * rows :, :] = jnp.dot(jnp.concatenate(left, axis=1), ops[...], preferred_element_type=jnp.float32)
 
     def message(t, n, slot, to):
         return pltpu.make_async_remote_copy(
@@ -191,7 +191,7 @@
 
     def pass_on(t, n, add):
         slot, to = route(t)
-        if t < near:
+        if add or t < near:
             total = product(t, n)
         else:
             total = acc[(t - near) * rows : (t - near + 1) * rows, starts[n] : starts[n] + widths[n]]
@@ -238,7 +238,7 @@
             if n > 0 and near > 1:
                 pass_on(1, n, False)
         parts(*late)
-        multiply_near()
+        multiply_from(near)
         for t, n in tail:
             pass_on(t, n, False)
 
@@ -262,23 +262,21 @@
                 ready_slab(n)
                 if n == 0:
                     wait_parts(0)
+                elif n < L - 1:
+                    parts(n)
+                pass_on(0, n, True)
                 if n == N - 1:
-                    parts(*late)
-                    multiply_near()
-                    if N > 2:
-                        pass_on(1, N - 3, True)
-                pass_on(0, n, True)
-                if n == 0:
-                    parts(1)
-                elif n < N - 1 and n > 1:
-                    pass_on(1, n - 2, True)
-            order = [(1, n) for n in range(max(N - 2, 0), N)]
-            for i, (t, n) in enumerate(tail):
-                if i < len(order):
-                    pass_on(*order[i], True)
-                pass_on(t, n, True)
-            for t, n in order[len(tail) :]:
-                pass_on(t, n, True)
+                    parts(*range(N, L - 1))
+                elif n < 2:
+                    continue
+                first = 0 if n == min(2, N - 1) else n - 1
+                for m in range(first, min(n, N - 1)):
+                    for t in range(1, L - 1):
+                        pass_on(t, m, True)
+            parts(L - 1)
+            multiply_from(L - 1)
+            for t in range(1, L - 1):
+                pass_on(t, N - 1, True)
             for n in range(N):
                 finish(n, True, True)
 

time: 36.2 us -> 37.1 us (1.025)
  Pallas kernels: 34.3 us -> 35.3 us
    pallas_call x1, Pallas kernels: 34.3 us -> 35.3 us  [shards(): pl.pallas_call(functools.partial(kernel, (R, C, L), widths), out_shape=ja...]
where the time goes in v6:
time: 37.1 us; the launch traced here: 37 us
  Pallas kernels  35.3 us (95%)
  local copies, waits for them, and re-layouts  1.67 us (5%)
    pallas_call x1, Pallas kernels, shards(): pl.pallas_call(functools.partial(kernel, (R, C, L), widths), out_shape=ja...  35.3 us
    unnamed x1, local copies, waits for them, and re-layouts  1.67 us

profile of v6, /device:TPU:0, one launch (start us, length us, event | category | flops | bytes accessed | tf_op | source)
XLA Modules:
  0.0 37.0 jit_solution(9964992466351119877)
XLA Ops:
  0.0 35.3 %shard_map.55 = bf16[256,512]{1,0:T(8,128)(2,1)} custom-call(bf16[1024,256]{1,0:T(8,128)(2,1)} %bitcast.4, s32[2,8]{1,0:T(2,128)} %bitcast.5, bf16[1,4,128,512]{3,2,1,0:T(8,128)(2,1)} %slab_hbm.1, s32[1,8]{1,0:T(1,128)} %owner_hbm.1, s32[2,4]{1,0:T(2,128)} %out_hbm.1), custom_call_target="tpu_custom_call" | custom-call | tf_op jit(solution)/shard_map/pallas_call | solution.py:310
  35.3 1.7 %copy.7 = bf16[256,512]{1,0:T(8,128)(2,1)} copy(bf16[256,512]{1,0:T(8,128)(2,1)} %shard_map.55) | data formatting | bytes 524288

commit v7 on v6

--- a/solution.py
+++ b/solution.py
@@ -234,9 +234,9 @@
             pass_on(0, n, False)
             if n == 1 and near > 1:
                 parts(1)
-                pass_on(1, 0, False)
-            if n > 0 and near > 1:
-                pass_on(1, n, False)
+            if near > 1:
+                for m in {1: (0, 1), N - 1: range(2, N)}.get(n, ()):
+                    pass_on(1, m, False)
         parts(*late)
         multiply_from(near)
         for t, n in tail:
@@ -262,21 +262,21 @@
                 ready_slab(n)
                 if n == 0:
                     wait_parts(0)
-                elif n < L - 1:
+                elif n < L:
                     parts(n)
+                if n == N - 1:
+                    parts(*range(N, L))
+                    pass_on(1, n - 1, True)
+                    multiply_from(L - 1)
                 pass_on(0, n, True)
-                if n == N - 1:
-                    parts(*range(N, L - 1))
-                elif n < 2:
-                    continue
-                first = 0 if n == min(2, N - 1) else n - 1
-                for m in range(first, min(n, N - 1)):
-                    for t in range(1, L - 1):
-                        pass_on(t, m, True)
-            parts(L - 1)
-            multiply_from(L - 1)
-            for t in range(1, L - 1):
-                pass_on(t, N - 1, True)
+                if n == N - 2:
+                    for m in range(n):
+                        for t in range(1, L - 1):
+                            pass_on(t, m, True)
+            pass_on(1, N - 1, True)
+            for n in (N - 2, N - 1):
+                for t in range(2, L - 1):
+                    pass_on(t, n, True)
             for n in range(N):
                 finish(n, True, True)
 

time: 37.1 us -> 37.1 us (level)
  no operation moved by 1% of the time
where the time goes in v7:
time: 37.1 us; the launch traced here: 36.9 us
  Pallas kernels  35.3 us (95%)
  local copies, waits for them, and re-layouts  1.67 us (5%)
    pallas_call x1, Pallas kernels, shards(): pl.pallas_call(functools.partial(kernel, (R, C, L), widths), out_shape=ja...  35.3 us
    unnamed x1, local copies, waits for them, and re-layouts  1.67 us

profile of v7, /device:TPU:0, one launch (start us, length us, event | category | flops | bytes accessed | tf_op | source)
XLA Modules:
  0.0 36.9 jit_solution(9035478046799950910)
XLA Ops:
  0.0 35.3 %shard_map.55 = bf16[256,512]{1,0:T(8,128)(2,1)} custom-call(bf16[1024,256]{1,0:T(8,128)(2,1)} %bitcast.4, s32[2,8]{1,0:T(2,128)} %bitcast.5, bf16[1,4,128,512]{3,2,1,0:T(8,128)(2,1)} %slab_hbm.1, s32[1,8]{1,0:T(1,128)} %owner_hbm.1, s32[2,4]{1,0:T(2,128)} %out_hbm.1), custom_call_target="tpu_custom_call" | custom-call | tf_op jit(solution)/shard_map/pallas_call | solution.py:310
  35.3 1.7 %copy.7 = bf16[256,512]{1,0:T(8,128)(2,1)} copy(bf16[256,512]{1,0:T(8,128)(2,1)} %shard_map.55) | data formatting | bytes 524288

commit v8 on v5

--- a/solution.py
+++ b/solution.py
@@ -273,11 +273,7 @@
                 elif n < N - 1 and n > 1:
                     pass_on(1, n - 2, True)
             order = [(1, n) for n in range(max(N - 2, 0), N)]
-            for i, (t, n) in enumerate(tail):
-                if i < len(order):
-                    pass_on(*order[i], True)
-                pass_on(t, n, True)
-            for t, n in order[len(tail) :]:
+            for t, n in order + tail:
                 pass_on(t, n, True)
             for n in range(N):
                 finish(n, True, True)
@@ -338,7 +334,7 @@
                 dma((2 * L, N)),
             ],
             compiler_params=pltpu.CompilerParams(
-                collective_id=0, has_side_effects=True, vmem_limit_bytes=56 * 2**20),
+                collective_id=0, has_side_effects=True, vmem_limit_bytes=int(53.4 * 2**20)),
         )(panel.reshape(panel.shape[0], depth), in_pat[:, 0, :].T, slab, owner, out_pat)
 
     in_specs = (

time: 36.2 us -> 36.1 us (level)
  the two profiles are of different devices: /device:TPU:0 before, /device:TPU:16 now
where the time goes in v8:
time: 36.1 us; the launch traced here: 36 us
  Pallas kernels  34.5 us (96%)
  local copies, waits for them, and re-layouts  1.4 us (4%)
    pallas_call x1, Pallas kernels, shards(): pl.pallas_call(functools.partial(kernel, (R, C, L), widths), out_shape=ja...  34.5 us
    unnamed x7, local copies, waits for them, and re-layouts  1.4 us

profile of v8, /device:TPU:16, one launch (start us, length us, event | category | flops | bytes accessed | tf_op | source)
XLA Modules:
  0.0 36.0 jit_solution(13523077082313002243)
XLA Ops:
  0.0 0.0 copy-start.1
  0.0 0.0 copy-start
  0.0 0.0 copy-start.2
  0.0 0.7 %copy-done.1 = s32[2,4]{1,0:T(2,128)S(1)} copy-done((s32[2,4]{1,0:T(2,128)S(1)}, s32[2,4]{1,0:T(2,128)}, u32[]{:S(2)}) %copy-start.1) | copy-done | bytes 56
  0.7 0.0 copy-done
  0.7 0.0 copy-done.2
  0.7 34.5 %shard_map.55 = bf16[256,512]{1,0:T(8,128)(2,1)S(1)} custom-call(bf16[1024,256]{1,0:T(8,128)(2,1)} %bitcast.5, s32[2,8]{1,0:T(2,128)S(1)} %bitcast.4, bf16[1,4,128,512]{3,2,1,0:T(8,128)(2,1)} %slab_hbm.1, s32[1,8]{1,0:T(1,128)S(1)} %copy-done.2, s32[2,4]{1,0:T(2,128)S(1)} %copy-done.1), custom_call_target="tpu_custom_call" | custom-call | tf_op jit(solution)/shard_map/pallas_call | solution.py:308
  35.2 0.7 %copy.7 = bf16[256,512]{1,0:T(8,128)(2,1)} copy(bf16[256,512]{1,0:T(8,128)(2,1)S(1)} %shard_map.55) | data formatting | bytes 524288
Async XLA Ops:
  0.0 0.7 %copy-start.1 = (s32[2,4]{1,0:T(2,128)S(1)}, s32[2,4]{1,0:T(2,128)}, u32[]{:S(2)}) copy-start(s32[2,4]{1,0:T(2,128)} %out_hbm.1) | copy-start | bytes 100
  0.0 0.7 %copy-start = (s32[8,1,2]{0,2,1:T(2,128)S(1)}, s32[8,1,2]{0,2,1:T(2,128)}, u32[]{:S(2)}) copy-start(s32[8,1,2]{0,2,1:T(2,128)} %param.6) | copy-start | bytes 196
  0.0 0.7 %copy-start.2 = (s32[1,8]{1,0:T(1,128)S(1)}, s32[1,8]{1,0:T(1,128)}, u32[]{:S(2)}) copy-start(s32[1,8]{1,0:T(1,128)} %owner_hbm.1) | copy-start | bytes 100

commit v9 on v5

--- a/solution.py
+++ b/solution.py
@@ -338,7 +338,7 @@
                 dma((2 * L, N)),
             ],
             compiler_params=pltpu.CompilerParams(
-                collective_id=0, has_side_effects=True, vmem_limit_bytes=56 * 2**20),
+                collective_id=0, has_side_effects=True, vmem_limit_bytes=int(53.4 * 2**20)),
         )(panel.reshape(panel.shape[0], depth), in_pat[:, 0, :].T, slab, owner, out_pat)
 
     in_specs = (

time: 36.2 us -> 35.2 us (0.972)
  Pallas kernels: 34.3 us -> 33.7 us
    pallas_call x1, Pallas kernels: 34.3 us -> 33.7 us  [shards(): pl.pallas_call(functools.partial(kernel, (R, C, L), widths), out_shape=ja...]
    unnamed x1 -> x7, local copies, waits for them, and re-layouts: 1.67 us -> 1.4 us
where the time goes in v9:
time: 35.2 us; the launch traced here: 35.1 us
  Pallas kernels  33.7 us (96%)
  local copies, waits for them, and re-layouts  1.4 us (4%)
    pallas_call x1, Pallas kernels, shards(): pl.pallas_call(functools.partial(kernel, (R, C, L), widths), out_shape=ja...  33.7 us
    unnamed x7, local copies, waits for them, and re-layouts  1.4 us

profile of v9, /device:TPU:0, one launch (start us, length us, event | category | flops | bytes accessed | tf_op | source)
XLA Modules:
  0.0 35.1 jit_solution(6866683882467609515)
XLA Ops:
  0.0 0.0 copy-start.1
  0.0 0.0 copy-start
  0.0 0.0 copy-start.2
  0.0 0.7 %copy-done.1 = s32[2,4]{1,0:T(2,128)S(1)} copy-done((s32[2,4]{1,0:T(2,128)S(1)}, s32[2,4]{1,0:T(2,128)}, u32[]{:S(2)}) %copy-start.1) | copy-done | bytes 56
  0.7 0.0 copy-done
  0.7 0.0 copy-done.2
  0.7 33.7 %shard_map.55 = bf16[256,512]{1,0:T(8,128)(2,1)S(1)} custom-call(bf16[1024,256]{1,0:T(8,128)(2,1)} %bitcast.5, s32[2,8]{1,0:T(2,128)S(1)} %bitcast.4, bf16[1,4,128,512]{3,2,1,0:T(8,128)(2,1)} %slab_hbm.1, s32[1,8]{1,0:T(1,128)S(1)} %copy-done.2, s32[2,4]{1,0:T(2,128)S(1)} %copy-done.1), custom_call_target="tpu_custom_call" | custom-call | tf_op jit(solution)/shard_map/pallas_call | solution.py:312
  34.4 0.7 %copy.7 = bf16[256,512]{1,0:T(8,128)(2,1)} copy(bf16[256,512]{1,0:T(8,128)(2,1)S(1)} %shard_map.55) | data formatting | bytes 524288
Async XLA Ops:
  0.0 0.7 %copy-start.1 = (s32[2,4]{1,0:T(2,128)S(1)}, s32[2,4]{1,0:T(2,128)}, u32[]{:S(2)}) copy-start(s32[2,4]{1,0:T(2,128)} %out_hbm.1) | copy-start | bytes 100
  0.0 0.7 %copy-start = (s32[8,1,2]{0,2,1:T(2,128)S(1)}, s32[8,1,2]{0,2,1:T(2,128)}, u32[]{:S(2)}) copy-start(s32[8,1,2]{0,2,1:T(2,128)} %param.6) | copy-start | bytes 196
  0.0 0.7 %copy-start.2 = (s32[1,8]{1,0:T(1,128)S(1)}, s32[1,8]{1,0:T(1,128)}, u32[]{:S(2)}) copy-start(s32[1,8]{1,0:T(1,128)} %owner_hbm.1) | copy-start | bytes 100
